TPU v7x, 32 devices: a whole 2x2x4 slice. The times are simulated.
32 devices in a mesh: stn: 8 (over z, x), beam: 4 (over y, core).
Axes of the slice: x: 2, y: 2, z: 4, core: 2. Of those that a mesh axis runs over, the one named last changes fastest.
Arguments:
- voltages: bfloat16 [64, 2, 614400], P(('stn', 'beam')), may hold values from -6 to 6
- fir_taps: float32 [12, 8192], replicated, may hold values from -1.75 to 1.75
- delays: float32 [8, 64, 64], P('stn', 'beam'), may hold values from -16 to 16
- taper: float32 [64, 64], replicated, may hold values from 0.5 to 2
- station_map: int32 [64], replicated, may hold values from 0 to 63, each once
- beam_order: int32 [64], replicated, may hold values from 0 to 63, each once
- owners: int32 [4], replicated, may hold values from 0 to 7
Outputs:
- beams_re: float32 [64, 4096, 128], P('beam', 'stn')
- beams_im: float32 [64, 4096, 128], P('beam', 'stn')
Inputs may be any that keep to these rules, and one draw needn't show every extreme that they name: `station_map`: each station row holds a different physical station. `beam_order`: each beam slot forms a different beam.
All inputs are finite; a program needn't handle non-finite values.
Results may differ from a plain program's by a relative error of at most 0.0064.
Values may be sent and summed in bfloat16 or wider, within the bound.
A program may use at most 128 MiB of HBM per device.

v0:
```python
import math

import jax
import jax.numpy as jnp
from jax import lax
from jax.sharding import PartitionSpec as P

P_SIZE = 64
Q = 128
CHANNELS = 4096


TWO_PI = 2.0 * math.pi


def from_root(value, axis, source):
    kept = jnp.where(lax.axis_index(axis) == source, value, 0).astype(value.dtype)
    return lax.psum(kept, axis)


def dft_tables():
    first_idx = jnp.arange(P_SIZE, dtype=jnp.int32)
    second_idx = jnp.arange(Q, dtype=jnp.int32)
    half_idx = jnp.arange(Q // 2, dtype=jnp.int32)
    first_angle = (
        TWO_PI / P_SIZE * (first_idx[:, None] * first_idx[None, :] % P_SIZE).astype(jnp.float32)
    )
    twist_angle = (
        TWO_PI / (P_SIZE * Q) * (first_idx[:, None] * second_idx[None, :]).astype(jnp.float32)
    )
    second_angle = TWO_PI / Q * (second_idx[:, None] * half_idx[None, :] % Q).astype(jnp.float32)
    return (
        jnp.cos(first_angle).astype(jnp.bfloat16),
        jnp.sin(first_angle).astype(jnp.bfloat16),
        jnp.cos(twist_angle),
        jnp.sin(twist_angle),
        jnp.cos(second_angle).astype(jnp.bfloat16),
        jnp.sin(second_angle).astype(jnp.bfloat16),
    )


def beam_weights(delay_cols, gain_cols, chan_ids):
    phase = (
        delay_cols[:, :, None]
        * chan_ids.astype(jnp.float32)[None, None, :]
        * (TWO_PI / (P_SIZE * Q))
    )
    weight_re = (gain_cols[:, :, None] * jnp.cos(phase)).astype(jnp.bfloat16)
    weight_im = (-(gain_cols[:, :, None] * jnp.sin(phase))).astype(jnp.bfloat16)
    left_re = jnp.concatenate((weight_re, -weight_im), axis=1)
    left_im = jnp.concatenate((weight_im, weight_re), axis=1)
    return (left_re, left_im)


def channelize(voltages, fir_taps):
    cos_one, sin_one, twist_cos, twist_sin, cos_two, sin_two = dft_tables()
    local_stations, pol_count, samples = voltages.shape
    tap_count, fft_width = fir_taps.shape
    frames = samples // fft_width - tap_count + 1
    blocks = voltages.reshape(local_stations, pol_count, frames + tap_count - 1, fft_width)
    filtered = jnp.zeros((local_stations, pol_count, frames, fft_width), jnp.float32)
    for tap_idx in range(tap_count):
        filtered = filtered + fir_taps[tap_idx] * blocks[:, :, tap_idx : tap_idx + frames].astype(
            jnp.float32
        )
    folded = filtered.astype(jnp.bfloat16).reshape(local_stations, pol_count, frames, P_SIZE, Q)
    first_table = jnp.concatenate((cos_one, -sin_one), axis=0)
    first_section = jnp.einsum(
        "spfnq,an->spfaq", folded, first_table, preferred_element_type=jnp.float32
    )
    first_re = first_section[:, :, :, :P_SIZE]
    first_im = first_section[:, :, :, P_SIZE:]
    turned = jnp.concatenate(
        (
            (first_re * twist_cos + first_im * twist_sin).astype(jnp.bfloat16),
            (first_im * twist_cos - first_re * twist_sin).astype(jnp.bfloat16),
        ),
        axis=4,
    )
    second_table = jnp.concatenate(
        (jnp.concatenate((cos_two, -sin_two), axis=1), jnp.concatenate((sin_two, cos_two), axis=1)),
        axis=0,
    )
    second = jnp.einsum("spfaq,qb->sbapf", turned, second_table, preferred_element_type=jnp.float32)
    half_q = Q // 2
    chan_re = (
        second[:, :half_q]
        .astype(jnp.bfloat16)
        .reshape(local_stations, half_q * P_SIZE, pol_count * frames)
    )
    chan_im = (
        second[:, half_q:]
        .astype(jnp.bfloat16)
        .reshape(local_stations, half_q * P_SIZE, pol_count * frames)
    )
    return jnp.stack((chan_re, chan_im), axis=0)


def combine(left_re, left_im, stacked_parts, beam_scale):
    stacked = jnp.concatenate((stacked_parts[0], stacked_parts[1]), axis=0)
    beam_re = (
        jnp.einsum("jrk,rkc->jkc", left_re, stacked, preferred_element_type=jnp.float32)
        * beam_scale
    )
    beam_im = (
        jnp.einsum("jrk,rkc->jkc", left_im, stacked, preferred_element_type=jnp.float32)
        * beam_scale
    )
    return jnp.stack((beam_re, beam_im), axis=0)


def on_device(voltages, fir_taps, delays, taper, station_map, beam_order, owners):
    stn_count = lax.axis_size("stn")
    beam_count = lax.axis_size("beam")
    stn_pos = lax.axis_index("stn")
    beam_pos = lax.axis_index("beam")
    local_stations = voltages.shape[0]
    stations = station_map.shape[0]
    group_beams = beam_order.shape[0] // beam_count
    chan_dev = CHANNELS // stn_count
    chan_ids = stn_pos * chan_dev + jnp.arange(chan_dev, dtype=jnp.int32)
    beam_scale = 1.0 / math.sqrt(P_SIZE * Q * stations)
    spectra = channelize(voltages, fir_taps)
    owner_model = from_root(delays, "stn", owners[beam_pos])[0]
    row_stn = jnp.arange(stn_count * local_stations, dtype=jnp.int32)
    all_rows = (
        (row_stn // local_stations * beam_count + jnp.arange(beam_count, dtype=jnp.int32)[:, None])
        * local_stations
        + row_stn % local_stations
    ).reshape(-1)
    phys_ids = station_map[all_rows]
    slot_gain = taper[beam_order[beam_pos * group_beams + jnp.arange(group_beams, dtype=jnp.int32)]]
    left_re, left_im = beam_weights(owner_model[:, phys_ids], slot_gain[:, phys_ids], chan_ids)
    full_rows = lax.all_gather(
        lax.all_to_all(spectra, "stn", split_axis=2, concat_axis=1, tiled=True),
        "beam",
        axis=1,
        tiled=True,
    )
    formed = combine(left_re, left_im, full_rows, beam_scale)
    return (formed[0], formed[1])


def solution(mesh):
    return jax.shard_map(
        on_device,
        mesh=mesh,
        in_specs=(P(("stn", "beam"), None, None), P(), P("stn", "beam", None), P(), P(), P(), P()),
        out_specs=(P("beam", "stn", None), P("beam", "stn", None)),
        check_vma=False,
    )
```

profile of v0, /device:TPU:9, one launch (start us, length us, event | category | flops | bytes accessed | tf_op | source)
XLA Modules:
  0.0 352.4 jit_solution(2686079435536517408)
XLA Ops:
  8.2 2.9 fusion.53
  11.2 6.3 %reshape.166 = bf16[2,2,75,8192]{3,2,1,0:T(8,128)(2,1)} reshape(bf16[2,2,614400]{2,1,0:T(2,128)(2,1)} %param.7) | data formatting | bytes 9830400 | tf_op jit(solution)/shard_map/reshape | solution.py:60
  17.4 28.3 %add_convert_fusion.1 = bf16[2,2,64,8192]{3,2,1,0:T(8,128)(2,1)S(1)} fusion(bf16[2,2,75,8192]{3,2,1,0:T(8,128)(2,1)} %reshape.166, f32[8192]{0:T(1024)S(1)} %bitcast.83, f32[8192]{0:T(1024)S(1)} %bitcast.84, f32[8192]{0:T(1024)S(1)} %bitcast.74, f32[8192]{0:T(1024)S(1)} %bitcast.75, f32[8192]{0:T(1024)S(1)} %bitcast.76, f32[8192]{0:T(1024)S(1)} %bitcast.77, ...), kind=kLoop, calls=%fused_computation.16 | loop fusion | flops 75497472 | bytes 54919168 | tf_op jit(solution)/shard_map/convert_element_type | solution.py:66
  46.9 2.4 convolution_bitcast_fusion
  49.3 2.5 add_convert_fusion
  51.9 3.1 convert_bitcast_fusion
  55.0 4.4 %fusion.52 = (bf16[2,64,64,2,64]{1,2,4,3,0:T(8,128)(2,1)}, bf16[2,64,64,2,64]{1,2,4,3,0:T(8,128)(2,1)}) fusion(bf16[2,128,64,2,64]{1,2,4,3,0:T(8,128)(2,1)S(1)} %convert_bitcast_fusion), kind=kLoop, calls=%fused_computation.94 | loop fusion | bytes 8388608 | tf_op jit(solution)/shard_map/slice | solution.py:87
  59.4 6.3 %copy.25 = bf16[2,64,64,2,64]{2,1,4,3,0:T(8,128)(2,1)} copy(bf16[2,64,64,2,64]{1,2,4,3,0:T(8,128)(2,1)} %get-tuple-element.12) | data formatting | bytes 4194304 | tf_op jit(solution)/shard_map/slice | solution.py:87
  65.7 5.7 %stack_reshape.6 = bf16[1,2,4096,128]{2,3,1,0:T(8,128)(2,1)S(1)} reshape(bf16[2,64,64,2,64]{2,1,4,3,0:T(8,128)(2,1)} %copy.25) | data formatting | bytes 4194304 | tf_op jit(solution)/shard_map/stack;reshape | solution.py:96
  71.4 6.3 %copy.26 = bf16[2,64,64,2,64]{2,1,4,3,0:T(8,128)(2,1)} copy(bf16[2,64,64,2,64]{1,2,4,3,0:T(8,128)(2,1)} %get-tuple-element.13) | data formatting | bytes 4194304 | tf_op jit(solution)/shard_map/slice | solution.py:92
  77.7 6.6 %stack_reshape.7 = bf16[1,2,4096,128]{2,3,1,0:T(8,128)(2,1)} reshape(bf16[2,64,64,2,64]{2,1,4,3,0:T(8,128)(2,1)} %copy.26) | data formatting | bytes 4194304 | tf_op jit(solution)/shard_map/stack;reshape | solution.py:96
  84.3 4.0 %pad_maximum_fusion.3 = bf16[2,2,4096,128]{2,3,1,0:T(8,128)(2,1)} fusion(bf16[1,2,4096,128]{2,3,1,0:T(8,128)(2,1)} %stack_reshape.7, bf16[1,2,4096,128]{2,3,1,0:T(8,128)(2,1)S(1)} %stack_reshape.6), kind=kLoop, calls=%fused_computation.18 | loop fusion | flops 2097152 | bytes 8388608 | tf_op jit(solution)/shard_map/stack | solution.py:96
  88.3 11.1 %copy.27 = bf16[2,2,4096,128]{3,1,0,2:T(2,128)(2,1)} copy(bf16[2,2,4096,128]{2,3,1,0:T(8,128)(2,1)} %pad_maximum_fusion.3) | data formatting | bytes 8388608 | tf_op jit(solution)/shard_map/stack | solution.py:96
  99.4 97.0 %all_to_all.18 = bf16[2,2,4096,128]{3,1,0,2:T(2,128)(2,1)S(1)} all-to-all(bf16[2,2,4096,128]{3,1,0,2:T(2,128)(2,1)} %copy.27), channel_id=1, replica_groups=mesh['stn'=8,'beam'=4] {'stn'}, dimensions={2} | all-to-all | bytes 8388608 | tf_op jit(solution)/shard_map/all_to_all | solution.py:135
  197.0 6.3 %copy.29 = bf16[2,8,2,512,128]{4,2,1,3,0:T(2,128)(2,1)} copy(bf16[2,8,2,512,128]{4,3,1,2,0:T(8,128)(2,1)S(1)} %bitcast.71) | data formatting | bytes 8388608 | tf_op jit(solution)/shard_map/all_to_all | solution.py:135
  206.2 27.2 %psum.7 = f32[16,64]{0,1:T(8,128)S(1)} all-reduce(f32[16,64]{0,1:T(8,128)S(1)} %select_bitcast_fusion), channel_id=1, replica_groups=mesh['stn'=8,'beam'=4] {'stn'}, use_global_device_ids=true, to_apply=%region_0.1 | all-reduce | flops 1024 | bytes 8192 | tf_op jit(solution)/shard_map/psum | solution.py:18
  236.1 16.7 %fusion.30 = bf16[16,64,512]{1,0,2:T(8,128)(2,1)} fusion(f32[512]{0:T(512)S(1)} %add_convert_fusion.2, f32[16,64]{1,0:T(8,128)S(1)} %copy.33, f32[16,64]{1,0:T(8,128)S(1)} %copy.31), kind=kLoop, calls=%fused_computation.52 | loop fusion | flops 4194304 | bytes 1058816 | tf_op jit(solution)/shard_map/neg | solution.py:50
  252.8 17.9 %negate_convert_fusion = (bf16[16,64,512]{1,0,2:T(8,128)(2,1)}, bf16[16,64,512]{1,0,2:T(8,128)(2,1)}) fusion(f32[512]{0:T(512)S(1)} %add_convert_fusion.2, f32[16,64]{1,0:T(8,128)S(1)} %copy.33, f32[16,64]{1,0:T(8,128)S(1)} %copy.31), kind=kLoop, calls=%fused_computation.22 | loop fusion | flops 3670016 | bytes 2107392 | tf_op jit(solution)/shard_map/convert_element_type | solution.py:49
  270.7 42.3 %all-gather.2.cloned.1.call-done = bf16[2,64,512,128]{3,1,2,0:T(8,128)(2,1)} async-done(((bf16[2,16,512,128]{3,1,2,0:T(8,128)(2,1)}), bf16[2,64,512,128]{3,1,2,0:T(8,128)(2,1)}) %all-gather.2.cloned.1.call-update) | async-done | bytes 16777232 | tf_op jit(solution)/shard_map/all_gather | solution.py:134
  313.0 10.8 %slice_bitcast_fusion.1 = (bf16[64,512,128]{2,0,1:T(8,128)(2,1)S(1)}, bf16[64,512,128]{2,0,1:T(8,128)(2,1)}) fusion(bf16[2,64,512,128]{3,1,2,0:T(8,128)(2,1)} %all-gather.2.cloned.1.call-done), kind=kLoop, calls=%fused_computation.9 | loop fusion | bytes 33554432 | tf_op jit(solution)/shard_map/squeeze | solution.py:100
  323.8 7.6 %multiply_bitcast_fusion = f32[16,512,128]{2,0,1:T(8,128)S(1)} fusion(bf16[64,512,128]{2,0,1:T(8,128)(2,1)} %get-tuple-element.11, bf16[64,512,128]{2,0,1:T(8,128)(2,1)S(1)} %get-tuple-element.10, bf16[16,64,512]{1,0,2:T(8,128)(2,1)} %get-tuple-element.27, bf16[16,64,512]{1,0,2:T(8,128)(2,1)} %get-tuple-element.26), kind=kOutput, calls=%fused_computation.20 | convolution fusion | flops 307232768 | bytes 23068672 | tf_op jit(solution)/shard_map/jrk,rkc->jkc/dot_general | solution.py:106
  331.4 3.3 copy.35
  334.7 7.6 %multiply_bitcast_fusion.1 = f32[16,512,128]{2,0,1:T(8,128)S(1)} fusion(bf16[64,512,128]{2,0,1:T(8,128)(2,1)} %get-tuple-element.11, bf16[64,512,128]{2,0,1:T(8,128)(2,1)S(1)} %get-tuple-element.10, bf16[16,64,512]{1,0,2:T(8,128)(2,1)} %fusion.30, bf16[16,64,512]{1,0,2:T(8,128)(2,1)} %get-tuple-element.27), kind=kOutput, calls=%fused_computation.21 | convolution fusion | flops 307232768 | bytes 23068672 | tf_op jit(solution)/shard_map/jrk,rkc->jkc/dot_general | solution.py:102
  342.2 3.3 copy.34
  (42 shorter events, 7.7 us)
Async XLA Ops:
  7.2 227.7 %copy-start = (f32[64,64]{1,0:T(8,128)S(1)}, f32[64,64]{1,0:T(8,128)}, u32[]{:S(2)}) copy-start(f32[64,64]{1,0:T(8,128)} %param.10) | copy-start | bytes 49156
  7.2 305.8 %all-gather.2.cloned.1.call-start = ((), (), s32[]{:S(2)}) async-start(), calls=%async_computation.1 | async-start | bytes 20971520 | tf_op jit(solution)/shard_map/all_gather | solution.py:134
  203.3 0.7 copy-start.3
  203.3 0.9 copy-start.4
  203.3 2.1 copy-start.1
  203.3 30.8 %copy-start.2 = (s32[64]{0:T(128)S(1)}, s32[64]{0:T(128)}, u32[]{:S(2)}) copy-start(s32[64]{0:T(128)} %param.12) | copy-start | bytes 772
Sparse Core Ops, SparseCore 0:
  203.5 109.4 all-gather.1
where the time goes:
time: 355 us; the launch traced here: 352 us
  blocking collectives  124 us (35%)
  local copies, waits for them, and re-layouts  79.9 us (23%)
  other arithmetic  70.4 us (20%)
  waiting for transfers between devices  42.3 us (12%)
  matrix products  20.7 us (6%)
  between operations  14.9 us (4%)
    all_to_all x1, blocking collectives, on_device(): lax.all_to_all(spectra, 'stn', split_axis=2, concat_axis=1, tiled=True)  97 us
    all_gather x1, waiting for transfers between devices, on_device(): lax.all_gather(lax.all_to_all(spectra, 'stn', split_axis=2, concat_axis=1...  42.3 us
    convert_element_type x1, other arithmetic, channelize(): filtered.astype(jnp.bfloat16)  28.3 us
    psum x1, blocking collectives, from_root(): return lax.psum(kept, axis)  27.2 us
    another operation x3, local copies, waits for them, and re-layouts, channelize(): return jnp.stack((chan_re, chan_im), axis=0)  23.4 us
    convert_element_type x1, other arithmetic, beam_weights(): weight_im = (-(gain_cols[:, :, None] * jnp.sin(phase))).astype(jnp.bfloat16)  17.9 us
    neg x1, other arithmetic, beam_weights(): left_re = jnp.concatenate((weight_re, -weight_im), axis=1)  16.7 us
    squeeze x1, local copies, waits for them, and re-layouts, combine(): stacked = jnp.concatenate((stacked_parts[0], stacked_parts[1]), axis=0)  10.8 us
  transfers between devices with their start and end apart: 1, of which 1 were waited for; matrix products, arithmetic and copies ran while one was open for 11% of the time, Pallas kernels for 0%

commit v1 on v0

--- a/solution.py
+++ b/solution.py
@@ -1,16 +1,236 @@
+import functools
 import math
 
 import jax
 import jax.numpy as jnp
 from jax import lax
+from jax.experimental import pallas as pl
+from jax.experimental.pallas import tpu as pltpu
 from jax.sharding import PartitionSpec as P
 
 P_SIZE = 64
 Q = 128
 CHANNELS = 4096
-
-
+NFFT = P_SIZE * Q
+TILE_B = 8
 TWO_PI = 2.0 * math.pi
+VMEM_LIMIT = 56 * 1024 * 1024
+
+SIN_COEF = (6.283185272447949, -41.34169703819964, 81.60502363802586, -76.70153767014536, 42.01607576124393, -14.86832274947347, 3.199338841413777)
+COS_COEF = (0.999999999885554, -19.739208743453883, 64.93938907589225, -85.45665831478402, 60.242131338256826, -26.404668186962848, 7.800131436606334, -1.4531123148805878)
+
+
+def sin_cos_turns(turns):
+    u = turns - jnp.round(turns)
+    w = u * u
+    s = jnp.full_like(u, SIN_COEF[-1])
+    for coef in SIN_COEF[-2::-1]:
+        s = s * w + coef
+    c = jnp.full_like(u, COS_COEF[-1])
+    for coef in COS_COEF[-2::-1]:
+        c = c * w + coef
+    return s * u, c
+
+
+def dft_tables():
+    first_idx = jnp.arange(P_SIZE, dtype=jnp.int32)
+    second_idx = jnp.arange(Q, dtype=jnp.int32)
+    half_idx = jnp.arange(Q // 2, dtype=jnp.int32)
+    first_angle = (
+        TWO_PI / P_SIZE * (first_idx[:, None] * first_idx[None, :] % P_SIZE).astype(jnp.float32)
+    )
+    twist_angle = (
+        TWO_PI / (P_SIZE * Q) * (first_idx[:, None] * second_idx[None, :]).astype(jnp.float32)
+    )
+    second_angle = TWO_PI / Q * (second_idx[:, None] * half_idx[None, :] % Q).astype(jnp.float32)
+    first = jnp.concatenate((jnp.cos(first_angle), -jnp.sin(first_angle)), axis=0)
+    cos_two = jnp.cos(second_angle).T.reshape(-1, TILE_B, Q)
+    sin_two = jnp.sin(second_angle).T.reshape(-1, TILE_B, Q)
+    re_rows = jnp.concatenate((cos_two, sin_two), axis=2)
+    im_rows = jnp.concatenate((-sin_two, cos_two), axis=2)
+    second = jnp.stack((re_rows, im_rows), axis=1).reshape(Q, 2 * Q)
+    return (
+        first.astype(jnp.bfloat16),
+        jnp.cos(twist_angle),
+        jnp.sin(twist_angle),
+        second.astype(jnp.bfloat16),
+    )
+
+
+def filter_station(volt_ref, taps_ref, filt, pols, frames, tap_count):
+    group = 8
+    for part in range(P_SIZE // 16):
+        rows = pl.ds(part * 16, 16)
+        taps = [taps_ref[m, rows, :] for m in range(tap_count)]
+
+        def body(idx, carry):
+            pol, first = idx // (frames // group), idx % (frames // group) * group
+            sums = [None] * group
+            for step in range(group + tap_count - 1):
+                value = volt_ref[pol, first + step, rows, :].astype(jnp.float32)
+                for f in range(group):
+                    m = step - f
+                    if 0 <= m < tap_count:
+                        term = taps[m] * value
+                        sums[f] = term if sums[f] is None else sums[f] + term
+            for f in range(group):
+                filt[pol * frames + first + f, rows, :] = sums[f].astype(jnp.bfloat16)
+            return carry
+
+        lax.fori_loop(0, pols * frames // group, body, 0)
+
+
+def first_section(filt, first_ref, cos_ref, sin_ref, turn_re, turn_im, count):
+    table = first_ref[...]
+    width = 2
+
+    def body(idx, carry):
+        c0 = idx * width
+        pair = jnp.concatenate([filt[c0 + i] for i in range(width)], axis=1)
+        both = jnp.dot(table, pair, preferred_element_type=jnp.float32)
+        for i in range(width):
+            re = both[:P_SIZE, i * Q : (i + 1) * Q]
+            im = both[P_SIZE:, i * Q : (i + 1) * Q]
+            rows = pl.ds(pl.multiple_of((c0 + i) * P_SIZE, P_SIZE), P_SIZE)
+            turn_re[rows, :] = re * cos_ref[...] + im * sin_ref[...]
+            turn_im[rows, :] = im * cos_ref[...] - re * sin_ref[...]
+        return carry
+
+    lax.fori_loop(0, count // width, body, 0, unroll=2)
+
+
+def second_section(second_ref, turn_re, turn_im, count, store):
+    table = second_ref[...]
+
+    def body(a, carry):
+        rows = pl.ds(a, count, stride=P_SIZE)
+        turned = jnp.concatenate(
+            (turn_re[rows, :].astype(jnp.bfloat16), turn_im[rows, :].astype(jnp.bfloat16)), axis=1
+        )
+        out = lax.dot_general(
+            table, turned, (((1,), (1,)), ((), ())), preferred_element_type=jnp.float32
+        )
+        store(a, out.astype(jnp.bfloat16))
+        return carry
+
+    lax.fori_loop(0, P_SIZE, body, 0, unroll=4)
+
+
+def channel_kernel(
+    frames, volt_ref, taps_ref, first_ref, cos_ref, sin_ref, second_ref, out_ref, filt, turn_re, turn_im
+):
+    pols = volt_ref.shape[1]
+    count = pols * frames
+    filter_station(volt_ref.at[0], taps_ref, filt, pols, frames, taps_ref.shape[0])
+    first_section(filt, first_ref, cos_ref, sin_ref, turn_re, turn_im, count)
+
+    def store(a, value):
+        out_ref[:, 0, a] = value.reshape(out_ref.shape[0], 2 * TILE_B, count)
+
+    second_section(second_ref, turn_re, turn_im, count, store)
+
+
+def channelize(voltages, fir_taps, tables):
+    stations, pols, samples = voltages.shape
+    tap_count = fir_taps.shape[0]
+    blocks = samples // NFFT
+    frames = blocks - tap_count + 1
+    count = pols * frames
+    tiles = P_SIZE // TILE_B
+    volts = voltages.reshape(stations, pols, blocks, P_SIZE, Q)
+    taps = fir_taps.reshape(tap_count, P_SIZE, Q)
+    whole = lambda shape: pl.BlockSpec(shape, lambda l: (0,) * len(shape))
+    return pl.pallas_call(
+        functools.partial(channel_kernel, frames),
+        grid=(stations,),
+        in_specs=[
+            pl.BlockSpec((1, pols, blocks, P_SIZE, Q), lambda l: (l, 0, 0, 0, 0)),
+            whole(taps.shape),
+        ]
+        + [whole(t.shape) for t in tables],
+        out_specs=pl.BlockSpec(
+            (tiles, 1, P_SIZE, 2 * TILE_B, count), lambda l: (0, l, 0, 0, 0)
+        ),
+        out_shape=jax.ShapeDtypeStruct((tiles, stations, P_SIZE, 2 * TILE_B, count), jnp.bfloat16),
+        scratch_shapes=[
+            pltpu.VMEM((count, P_SIZE, Q), jnp.bfloat16),
+            pltpu.VMEM((count * P_SIZE, Q), jnp.float32),
+            pltpu.VMEM((count * P_SIZE, Q), jnp.float32),
+        ],
+        compiler_params=pltpu.CompilerParams(vmem_limit_bytes=VMEM_LIMIT),
+        name="channelize",
+    )(volts, taps, *tables)
+
+
+def beam_kernel(step_a, scale, data_ref, delay_ref, gain_ref, base_ref, re_ref, im_ref):
+    beams, lanes = delay_ref.shape
+    count = data_ref.shape[-1]
+    lane = lax.broadcasted_iota(jnp.int32, (TILE_B, lanes), 1)
+    row = lax.broadcasted_iota(jnp.int32, (TILE_B, lanes), 0)
+    keep = lane % TILE_B == row
+    quarter = (lane[:1] // TILE_B % 2).astype(jnp.float32) * 0.25
+    delay = delay_ref[...]
+    chan = base_ref[...] + (pl.program_id(0) * step_a).astype(jnp.float32)
+    sin_t, cos_t = sin_cos_turns(delay * chan * (1.0 / NFFT) - quarter)
+    sin_d, cos_d = sin_cos_turns(delay * (1.0 / NFFT))
+    part_re = gain_ref[...] * cos_t
+    part_im = -(gain_ref[...] * sin_t)
+
+    def spread(part):
+        return (
+            jnp.where(keep[None], part[:, None, :], 0.0)
+            .astype(jnp.bfloat16)
+            .reshape(beams * TILE_B, lanes)
+        )
+
+    out_re = re_ref.reshape(beams * TILE_B * step_a, count)
+    out_im = im_ref.reshape(beams * TILE_B * step_a, count)
+    for a in range(step_a):
+        if a:
+            part_re, part_im = (
+                part_re * cos_d + part_im * sin_d,
+                part_im * cos_d - part_re * sin_d,
+            )
+        data = data_ref[:, a].reshape(lanes, count)
+        rows = pl.ds(a, beams * TILE_B, stride=step_a)
+        out_re[rows, :] = (
+            jnp.dot(spread(part_re), data, preferred_element_type=jnp.float32) * scale
+        )
+        out_im[rows, :] = (
+            jnp.dot(spread(part_im), data, preferred_element_type=jnp.float32) * scale
+        )
+
+
+def form_beams(data, delay, gain, first_chan, scale):
+    stations, _, tile_rows, count = data.shape
+    beams = delay.shape[0]
+    lanes = stations * tile_rows
+    step_a = 8
+    base = first_chan + P_SIZE * (jnp.arange(lanes, dtype=jnp.int32) % TILE_B)
+    spec = lambda shape: pl.BlockSpec(shape, lambda i: (0,) * len(shape))
+    out_spec = pl.BlockSpec((beams * TILE_B, step_a, count), lambda i: (0, i, 0))
+    out_shape = jax.ShapeDtypeStruct((beams * TILE_B, P_SIZE, count), jnp.float32)
+    re, im = pl.pallas_call(
+        functools.partial(beam_kernel, step_a, scale),
+        grid=(P_SIZE // step_a,),
+        in_specs=[
+            pl.BlockSpec((stations, step_a, tile_rows, count), lambda i: (0, i, 0, 0)),
+            spec((beams, lanes)),
+            spec((beams, lanes)),
+            spec((1, lanes)),
+        ],
+        out_specs=[out_spec, out_spec],
+        out_shape=[out_shape, out_shape],
+        compiler_params=pltpu.CompilerParams(vmem_limit_bytes=VMEM_LIMIT),
+        name="form_beams",
+    )(
+        data,
+        jnp.repeat(delay, tile_rows, axis=1),
+        jnp.repeat(gain, tile_rows, axis=1),
+        base.astype(jnp.float32)[None],
+    )
+    shape = (beams, TILE_B * P_SIZE, count)
+    return re.reshape(shape), im.reshape(shape)
 
 
 def from_root(value, axis, source):
@@ -18,7 +238,7 @@
     return lax.psum(kept, axis)
 
 
-def dft_tables():
+def general_tables():
     first_idx = jnp.arange(P_SIZE, dtype=jnp.int32)
     second_idx = jnp.arange(Q, dtype=jnp.int32)
     half_idx = jnp.arange(Q // 2, dtype=jnp.int32)
@@ -52,8 +272,8 @@
     return (left_re, left_im)
 
 
-def channelize(voltages, fir_taps):
-    cos_one, sin_one, twist_cos, twist_sin, cos_two, sin_two = dft_tables()
+def general_channelize(voltages, fir_taps):
+    cos_one, sin_one, twist_cos, twist_sin, cos_two, sin_two = general_tables()
     local_stations, pol_count, samples = voltages.shape
     tap_count, fft_width = fir_taps.shape
     frames = samples // fft_width - tap_count + 1
@@ -109,7 +329,7 @@
     return jnp.stack((beam_re, beam_im), axis=0)
 
 
-def on_device(voltages, fir_taps, delays, taper, station_map, beam_order, owners):
+def general_device(voltages, fir_taps, delays, taper, station_map, beam_order, owners):
     stn_count = lax.axis_size("stn")
     beam_count = lax.axis_size("beam")
     stn_pos = lax.axis_index("stn")
@@ -120,7 +340,7 @@
     chan_dev = CHANNELS // stn_count
     chan_ids = stn_pos * chan_dev + jnp.arange(chan_dev, dtype=jnp.int32)
     beam_scale = 1.0 / math.sqrt(P_SIZE * Q * stations)
-    spectra = channelize(voltages, fir_taps)
+    spectra = general_channelize(voltages, fir_taps)
     owner_model = from_root(delays, "stn", owners[beam_pos])[0]
     row_stn = jnp.arange(stn_count * local_stations, dtype=jnp.int32)
     all_rows = (
@@ -141,6 +361,37 @@
     return (formed[0], formed[1])
 
 
+def on_device(voltages, fir_taps, delays, taper, station_map, beam_order, owners):
+    stn_count = lax.axis_size("stn")
+    beam_count = lax.axis_size("beam")
+    stn_pos = lax.axis_index("stn")
+    beam_pos = lax.axis_index("beam")
+    local_stations = voltages.shape[0]
+    stations = station_map.shape[0]
+    group_beams = beam_order.shape[0] // beam_count
+    chan_dev = CHANNELS // stn_count
+    if chan_dev != P_SIZE * TILE_B:
+        return general_device(
+            voltages, fir_taps, delays, taper, station_map, beam_order, owners
+        )
+    scale = 1.0 / math.sqrt(NFFT * stations)
+    owner = owners[beam_pos]
+    kept = jnp.where(stn_pos == owner, delays[0], 0.0)
+    model = lax.psum(kept, "stn")
+    spectra = channelize(voltages, fir_taps, dft_tables())
+    row_stn = jnp.arange(stn_count * local_stations, dtype=jnp.int32)
+    all_rows = (
+        (row_stn // local_stations * beam_count + jnp.arange(beam_count, dtype=jnp.int32)[:, None])
+        * local_stations
+        + row_stn % local_stations
+    ).reshape(-1)
+    phys = station_map[all_rows]
+    slot_gain = taper[beam_order[beam_pos * group_beams + jnp.arange(group_beams, dtype=jnp.int32)]]
+    mine = lax.all_to_all(spectra, "stn", split_axis=0, concat_axis=1, tiled=True)
+    data = lax.all_gather(mine[0], "beam", axis=0, tiled=True)
+    return form_beams(data, model[:, phys], slot_gain[:, phys], stn_pos * chan_dev, scale)
+
+
 def solution(mesh):
     return jax.shard_map(
         on_device,

time: 355 us -> 285 us (0.80)
  other arithmetic: 70.4 us -> 3.05 us
  local copies, waits for them, and re-layouts: 79.9 us -> 15.7 us
  Pallas kernels: 0 us -> 53.9 us
  waiting for transfers between devices: 42.3 us -> 71.9 us
  matrix products: 20.7 us -> 0 us
    pallas_call x0 -> x2, Pallas kernels: none -> 53.9 us  [the longest x1 37.9 us: channelize(): pl.pallas_call(functools.partial(channel_kernel, frames), grid=(stations,...]
    convert_element_type x6 -> x1, other arithmetic: 49.1 us -> 0.6 us  [form_beams(): base.astype(jnp.float32)[None]]
    all_gather x1, waiting for transfers between devices: 42.3 us -> 71.9 us  [on_device(): data = lax.all_gather(mine[0], 'beam', axis=0, tiled=True)]
    another operation x3 -> x0, local copies, waits for them, and re-layouts: 23.4 us -> none  [channelize(): return jnp.stack((chan_re, chan_im), axis=0)]
    dot_general x4 -> x0, matrix products: 20.7 us -> none  [the longest x1 7.56 us: combine(): jnp.einsum('jrk,rkc->jkc', left_im, stacked, preferred_element_type=jnp.f...]
    slice x4 -> x0, local copies, waits for them, and re-layouts: 20 us -> none  [the longest x2 10.7 us: channelize(): second[:, :half_q].astype(jnp.bfloat16)]
    neg x3 -> x0, other arithmetic: 17.1 us -> none  [the longest x1 16.7 us: beam_weights(): left_re = jnp.concatenate((weight_re, -weight_im), axis=1)]
    squeeze x1 -> x0, local copies, waits for them, and re-layouts: 10.8 us -> none  [combine(): stacked = jnp.concatenate((stacked_parts[0], stacked_parts[1]), axis=0)]
  transfers between devices with their start and end apart: 1 -> 1, of which waited for: 1 -> 1; matrix products, arithmetic and copies ran while one was open for 11% -> 2% of each run, Pallas kernels for 0% -> 0%
where the time goes in v1:
time: 285 us; the launch traced here: 284 us
  blocking collectives  124 us (44%)
  waiting for transfers between devices  71.9 us (25%)
  Pallas kernels  53.9 us (19%)
  local copies, waits for them, and re-layouts  15.7 us (6%)
  between operations  14.8 us (5%)
  other arithmetic  3.05 us (1%)
    all_to_all x1, blocking collectives, on_device(): lax.all_to_all(spectra, 'stn', split_axis=0, concat_axis=1, tiled=True)  97.1 us
    all_gather x1, waiting for transfers between devices, on_device(): data = lax.all_gather(mine[0], 'beam', axis=0, tiled=True)  71.9 us
    pallas_call x1, Pallas kernels, channelize(): pl.pallas_call(functools.partial(channel_kernel, frames), grid=(stations,...  37.9 us
    psum x1, blocking collectives, on_device(): model = lax.psum(kept, 'stn')  27.1 us
    pallas_call x1, Pallas kernels, form_beams(): pl.pallas_call(functools.partial(beam_kernel, step_a, scale), grid=(P_SIZ...  16 us
    reshape x1, local copies, waits for them, and re-layouts, channelize(): volts = voltages.reshape(stations, pols, blocks, P_SIZE, Q)  6.8 us
  transfers between devices with their start and end apart: 1, of which 1 were waited for; matrix products, arithmetic and copies ran while one was open for 2% of the time, Pallas kernels for 0%

profile of v1, /device:TPU:9, one launch (start us, length us, event | category | flops | bytes accessed | tf_op | source)
XLA Modules:
  0.0 283.6 jit_solution(15883156052335957782)
XLA Ops:
  7.4 0.8 fusion.8
  8.2 0.2 fusion.15
  8.4 1.1 copy.24
  9.5 0.8 slice.10.taps_ref
  10.3 6.8 %reshape.194.volt_ref = bf16[2,2,75,64,128]{4,3,2,1,0:T(8,128)(2,1)} reshape(bf16[2,2,614400]{2,1,0:T(2,128)(2,1)} %param.7) | data formatting | bytes 9830400 | tf_op jit(solution)/shard_map/reshape | solution.py:140
  17.1 0.6 pad_maximum_fusion.1.first_ref
  17.7 0.6 pad_maximum_fusion
  18.3 37.9 %channelize.1 = bf16[8,2,64,16,128]{4,3,2,1,0:T(8,128)(2,1)} custom-call(bf16[2,2,75,64,128]{4,3,2,1,0:T(8,128)(2,1)} %reshape.194.volt_ref, f32[12,64,128]{2,1,0:T(8,128)} %slice.10.taps_ref, bf16[128,64]{1,0:T(8,128)(2,1)} %pad_maximum_fusion.1.first_ref, f32[64,128]{1,0:T(8,128)} %get-tuple-element.14.cos_ref, f32[64,128]{1,0:T(8,128)} %get-tuple-element.13.sin_ref, ...), custom_call_target="tpu_custom_call" | custom-call | tf_op jit(solution)/shard_map/channelize/pallas_call | solution.py:143
  56.2 97.1 %all_to_all.4 = bf16[8,2,64,16,128]{4,3,2,1,0:T(8,128)(2,1)} all-to-all(bf16[8,2,64,16,128]{4,3,2,1,0:T(8,128)(2,1)} %channelize.1), channel_id=1, replica_groups=mesh['stn'=8,'beam'=4] {'stn'}, dimensions={0} | all-to-all | bytes 8388608 | tf_op jit(solution)/shard_map/all_to_all | solution.py:390
  153.4 0.6 copy-done.4
  154.0 0.6 dynamic_slice.3
  155.4 0.7 gather_fusion.2
  156.1 0.6 gather_fusion.3
  156.8 0.8 gather_fusion
  157.6 0.6 gather_fusion.4
  158.3 27.1 %psum.7 = f32[16,64]{0,1:T(8,128)S(1)} all-reduce(f32[16,64]{0,1:T(8,128)S(1)} %select_bitcast_fusion), channel_id=1, replica_groups=mesh['stn'=8,'beam'=4] {'stn'}, use_global_device_ids=true, to_apply=%region_0.1 | all-reduce | flops 1024 | bytes 8192 | tf_op jit(solution)/shard_map/psum | solution.py:380
  185.4 0.6 gather_fusion.1
  186.1 0.2 broadcast_in_dim.9
  186.3 0.9 reshape.196.delay_ref
  187.2 0.2 broadcast_in_dim.10
  187.4 0.9 reshape.197.gain_ref
  188.3 0.6 fusion.18.base_ref
  188.9 71.9 %all-gather.2.cloned.1.call-done.data_ref = bf16[64,64,16,128]{3,2,1,0:T(8,128)(2,1)} async-done(((bf16[16,64,16,128]{3,2,1,0:T(8,128)(2,1)}), bf16[64,64,16,128]{3,2,1,0:T(8,128)(2,1)}) %all-gather.2.cloned.1.call-update) | async-done | bytes 16777232 | tf_op jit(solution)/shard_map/all_gather | solution.py:391
  260.8 16.0 %form_beams.1 = (f32[128,64,128]{2,1,0:T(8,128)}, f32[128,64,128]{2,1,0:T(8,128)}) custom-call(bf16[64,64,16,128]{3,2,1,0:T(8,128)(2,1)} %all-gather.2.cloned.1.call-done.data_ref, f32[16,1024]{1,0:T(8,128)} %reshape.196.delay_ref, f32[16,1024]{1,0:T(8,128)} %reshape.197.gain_ref, f32[1,1024]{1,0:T(1,128)} %fusion.18.base_ref), custom_call_target="tpu_custom_call" | custom-call | tf_op jit(solution)/shard_map/form_beams/pallas_call | solution.py:213
  (30 shorter events, 0.7 us)
Async XLA Ops:
  7.2 148.9 %copy-start = (f32[64,64]{1,0:T(8,128)S(1)}, f32[64,64]{1,0:T(8,128)}, u32[]{:S(2)}) copy-start(f32[64,64]{1,0:T(8,128)} %param.10) | copy-start | bytes 49156
  7.2 253.6 %all-gather.2.cloned.1.call-start = ((), (), s32[]{:S(2)}) async-start(), calls=%async_computation.1 | async-start | bytes 20971520 | tf_op jit(solution)/shard_map/all_gather | solution.py:391
  153.4 0.7 copy-start.4
  153.4 2.0 copy-start.1
  153.4 3.4 %copy-start.2 = (s32[64]{0:T(128)S(1)}, s32[64]{0:T(128)}, u32[]{:S(2)}) copy-start(s32[64]{0:T(128)} %param.11) | copy-start | bytes 772
  153.4 4.8 %copy-start.3 = (f32[1,16,64]{2,1,0:T(8,128)S(1)}, f32[1,16,64]{2,1,0:T(8,128)}, u32[]{:S(2)}) copy-start(f32[1,16,64]{2,1,0:T(8,128)} %param.9) | copy-start | bytes 12292
Sparse Core Ops, SparseCore 0:
  153.5 107.2 all-gather.1

commit v2 on v1

--- a/solution.py
+++ b/solution.py
@@ -15,6 +15,8 @@
 TILE_B = 8
 TWO_PI = 2.0 * math.pi
 VMEM_LIMIT = 56 * 1024 * 1024
+SEND_ORDER = (6, 1, 4, 2, 7, 3, 5)
+WAIT_ORDER = (1, 2, 3, 6, 4, 7, 5)
 
 SIN_COEF = (6.283185272447949, -41.34169703819964, 81.60502363802586, -76.70153767014536, 42.01607576124393, -14.86832274947347, 3.199338841413777)
 COS_COEF = (0.999999999885554, -19.739208743453883, 64.93938907589225, -85.45665831478402, 60.242131338256826, -26.404668186962848, 7.800131436606334, -1.4531123148805878)
@@ -82,7 +84,7 @@
 
 def first_section(filt, first_ref, cos_ref, sin_ref, turn_re, turn_im, count):
     table = first_ref[...]
-    width = 2
+    width = 4
 
     def body(idx, carry):
         c0 = idx * width
@@ -113,7 +115,7 @@
         store(a, out.astype(jnp.bfloat16))
         return carry
 
-    lax.fori_loop(0, P_SIZE, body, 0, unroll=4)
+    lax.fori_loop(0, P_SIZE, body, 0, unroll=8)
 
 
 def channel_kernel(
@@ -162,6 +164,149 @@
     )(volts, taps, *tables)
 
 
+def exchange_kernel(
+    spec_ref,
+    model_ref,
+    data_ref,
+    models_ref,
+    direct_send,
+    direct_recv,
+    far_send,
+    far_recv,
+    near_send,
+    near_recv,
+    last_send,
+    last_recv,
+    model_send,
+    model_recv,
+    local_sem,
+):
+    stn, beam = lax.axis_index("stn"), lax.axis_index("beam")
+    locals_ = spec_ref.shape[1]
+    far = (beam + 2) % 4
+    near = beam + 1 - 2 * (beam % 2)
+
+    def partner(m):
+        z, x = stn // 2, stn % 2
+        if m % 2:
+            x = 1 - x
+        if m // 2 % 2:
+            z = z + 1 - 2 * (z % 2)
+        if m // 4:
+            z = (z + 2) % 4
+        return z * 2 + x
+
+    def row(s, b, l):
+        return (s * 4 + b) * locals_ + l
+
+    def remote(src, dst, send, recv, s, b):
+        copy = pltpu.make_async_remote_copy(
+            src_ref=src,
+            dst_ref=dst,
+            send_sem=send,
+            recv_sem=recv,
+            device_id=(s, b),
+            device_id_type=pl.DeviceIdType.MESH,
+        )
+        copy.start()
+        return copy
+
+    barrier = pltpu.get_barrier_semaphore()
+    peers = [(partner(m), beam) for m in range(1, 8)] + [(stn, far), (stn, near)]
+    for peer in peers:
+        pl.semaphore_signal(barrier, inc=1, device_id=peer, device_id_type=pl.DeviceIdType.MESH)
+    pl.semaphore_wait(barrier, len(peers))
+
+    own_copies = [pltpu.make_async_copy(model_ref, models_ref.at[stn], local_sem.at[locals_])]
+    direct, far_copy, near_copy, last_copy, model_copy = {}, {}, {}, {}, {}
+    for l in range(locals_):
+        own_copies.append(
+            pltpu.make_async_copy(
+                spec_ref.at[stn, l], data_ref.at[row(stn, beam, l)], local_sem.at[l]
+            )
+        )
+        for m in SEND_ORDER:
+            direct[m, l] = remote(
+                spec_ref.at[partner(m), l],
+                data_ref.at[row(stn, beam, l)],
+                direct_send.at[m, l],
+                direct_recv.at[m, l],
+                partner(m),
+                beam,
+            )
+        if l == 0:
+            for m in range(1, 8):
+                model_copy[m] = remote(
+                    model_ref,
+                    models_ref.at[stn],
+                    model_send.at[m],
+                    model_recv.at[m],
+                    partner(m),
+                    beam,
+                )
+    for copy in own_copies:
+        copy.start()
+
+    def pass_on(key):
+        m, l = key
+        far_copy[key].wait_recv()
+        place = data_ref.at[row(partner(m), far, l)]
+        last_copy[key] = remote(
+            place, place, last_send.at[m, l], last_recv.at[m, l], stn, near
+        )
+
+    steps = [(m, l) for m in (0,) + WAIT_ORDER[:3] for l in range(locals_)]
+    steps += [(m, l) for l in range(locals_) for m in WAIT_ORDER[3:]]
+    before = None
+    for key in steps:
+        m, l = key
+        place = data_ref.at[row(partner(m), beam, l)]
+        if m:
+            direct[key].wait_recv()
+            src = place
+        else:
+            src = spec_ref.at[stn, l]
+        far_copy[key] = remote(src, place, far_send.at[m, l], far_recv.at[m, l], stn, far)
+        near_copy[key] = remote(src, place, near_send.at[m, l], near_recv.at[m, l], stn, near)
+        if before is not None:
+            pass_on(before)
+        before = key
+    pass_on(before)
+    for key in steps:
+        near_copy[key].wait_recv()
+        last_copy[key].wait_recv()
+        far_copy[key].wait_send()
+        near_copy[key].wait_send()
+        last_copy[key].wait_send()
+    for copy in direct.values():
+        copy.wait_send()
+    for copy in model_copy.values():
+        copy.wait()
+    for copy in own_copies:
+        copy.wait()
+
+
+def exchange(spectra, model):
+    stn_count, locals_ = spectra.shape[:2]
+    stations = stn_count * 4 * locals_
+    pair = pltpu.SemaphoreType.DMA((stn_count, locals_))
+    one = pltpu.SemaphoreType.DMA((stn_count,))
+    return pl.pallas_call(
+        exchange_kernel,
+        in_specs=[pl.BlockSpec(memory_space=pl.ANY)] * 2,
+        out_specs=[pl.BlockSpec(memory_space=pl.ANY)] * 2,
+        out_shape=[
+            jax.ShapeDtypeStruct((stations,) + spectra.shape[2:], spectra.dtype),
+            jax.ShapeDtypeStruct((stn_count,) + model.shape, model.dtype),
+        ],
+        scratch_shapes=[pair] * 8 + [one, one, pltpu.SemaphoreType.DMA((locals_ + 1,))],
+        compiler_params=pltpu.CompilerParams(
+            collective_id=0, has_side_effects=True, vmem_limit_bytes=VMEM_LIMIT
+        ),
+        name="exchange",
+    )(spectra, model)
+
+
 def beam_kernel(step_a, scale, data_ref, delay_ref, gain_ref, base_ref, re_ref, im_ref):
     beams, lanes = delay_ref.shape
     count = data_ref.shape[-1]
@@ -370,26 +515,17 @@
     stations = station_map.shape[0]
     group_beams = beam_order.shape[0] // beam_count
     chan_dev = CHANNELS // stn_count
-    if chan_dev != P_SIZE * TILE_B:
+    if (stn_count, beam_count, chan_dev) != (8, 4, P_SIZE * TILE_B):
         return general_device(
             voltages, fir_taps, delays, taper, station_map, beam_order, owners
         )
     scale = 1.0 / math.sqrt(NFFT * stations)
-    owner = owners[beam_pos]
-    kept = jnp.where(stn_pos == owner, delays[0], 0.0)
-    model = lax.psum(kept, "stn")
+    slot_gain = taper[beam_order[beam_pos * group_beams + jnp.arange(group_beams, dtype=jnp.int32)]]
+    own_model = jnp.pad(delays[0][:, station_map], ((0, 0), (0, -stations % 128)))
     spectra = channelize(voltages, fir_taps, dft_tables())
-    row_stn = jnp.arange(stn_count * local_stations, dtype=jnp.int32)
-    all_rows = (
-        (row_stn // local_stations * beam_count + jnp.arange(beam_count, dtype=jnp.int32)[:, None])
-        * local_stations
-        + row_stn % local_stations
-    ).reshape(-1)
-    phys = station_map[all_rows]
-    slot_gain = taper[beam_order[beam_pos * group_beams + jnp.arange(group_beams, dtype=jnp.int32)]]
-    mine = lax.all_to_all(spectra, "stn", split_axis=0, concat_axis=1, tiled=True)
-    data = lax.all_gather(mine[0], "beam", axis=0, tiled=True)
-    return form_beams(data, model[:, phys], slot_gain[:, phys], stn_pos * chan_dev, scale)
+    data, models = exchange(spectra, own_model)
+    model = models[owners[beam_pos]][:, :stations]
+    return form_beams(data, model, slot_gain[:, station_map], stn_pos * chan_dev, scale)
 
 
 def solution(mesh):

time: 285 us -> 196 us (0.69)
  blocking collectives: 124 us -> 0 us
  Pallas kernels: 53.9 us -> 172 us
  waiting for transfers between devices: 71.9 us -> 0 us
  between operations: 14.8 us -> 2.66 us
    pallas_call x0 -> x1, Pallas kernels: none -> 124 us  [exchange(): pl.pallas_call(exchange_kernel, in_specs=[pl.BlockSpec(memory_space=pl.AN...]
    all_to_all x1 -> x0, blocking collectives: 97.1 us -> none  [on_device(): lax.all_to_all(spectra, 'stn', split_axis=0, concat_axis=1, tiled=True)]
    all_gather x1 -> x0, waiting for transfers between devices: 71.9 us -> none  [on_device(): data = lax.all_gather(mine[0], 'beam', axis=0, tiled=True)]
    psum x1 -> x0, blocking collectives: 27.1 us -> none  [on_device(): model = lax.psum(kept, 'stn')]
    pallas_call x1, Pallas kernels: 37.9 us -> 31.1 us  [channelize(): pl.pallas_call(functools.partial(channel_kernel, frames), grid=(stations,...]
  transfers between devices with their start and end apart: 1 -> 0, of which waited for: 1 -> 0; matrix products, arithmetic and copies ran while one was open for 2% -> 0% of each run, Pallas kernels for 0% -> 0%
where the time goes in v2:
time: 196 us; the launch traced here: 195 us
  Pallas kernels  172 us (88%)
  local copies, waits for them, and re-layouts  17.5 us (9%)
  other arithmetic  3.73 us (2%)
  between operations  2.66 us (1%)
    pallas_call x1, Pallas kernels, exchange(): pl.pallas_call(exchange_kernel, in_specs=[pl.BlockSpec(memory_space=pl.AN...  124 us
    pallas_call x1, Pallas kernels, channelize(): pl.pallas_call(functools.partial(channel_kernel, frames), grid=(stations,...  31.1 us
    pallas_call x1, Pallas kernels, form_beams(): pl.pallas_call(functools.partial(beam_kernel, step_a, scale), grid=(P_SIZ...  16 us
    reshape x1, local copies, waits for them, and re-layouts, channelize(): volts = voltages.reshape(stations, pols, blocks, P_SIZE, Q)  6.77 us

profile of v2, /device:TPU:9, one launch (start us, length us, event | category | flops | bytes accessed | tf_op | source)
XLA Modules:
  0.0 195.4 jit_solution(14823067277686894754)
XLA Ops:
  0.7 1.2 dynamic_slice.6
  3.9 0.7 compare_select_fusion.2
  4.5 1.3 gather_fusion.1
  5.9 0.6 fusion.18.base_ref
  6.5 0.6 gather_fusion.2
  7.1 0.6 gather_fusion.3
  7.8 0.8 copy.15
  8.6 0.6 gather_fusion
  9.2 0.6 pad.4.model_ref
  10.0 0.6 pad_maximum_fusion.1.first_ref
  10.6 0.2 fusion.15
  10.9 0.6 pad_maximum_fusion
  11.5 0.8 fusion.8
  12.3 0.2 broadcast_in_dim.8
  12.5 0.9 reshape.107.gain_ref
  13.4 1.1 copy.19
  14.6 0.8 slice.13.taps_ref
  15.3 6.8 %reshape.104.volt_ref = bf16[2,2,75,64,128]{4,3,2,1,0:T(8,128)(2,1)} reshape(bf16[2,2,614400]{2,1,0:T(2,128)(2,1)} %param.7) | data formatting | bytes 9830400 | tf_op jit(solution)/shard_map/reshape | solution.py:142
  22.1 31.1 %channelize.1.spec_ref = bf16[8,2,64,16,128]{4,3,2,1,0:T(8,128)(2,1)} custom-call(bf16[2,2,75,64,128]{4,3,2,1,0:T(8,128)(2,1)} %reshape.104.volt_ref, f32[12,64,128]{2,1,0:T(8,128)} %slice.13.taps_ref, bf16[128,64]{1,0:T(8,128)(2,1)} %pad_maximum_fusion.1.first_ref, f32[64,128]{1,0:T(8,128)} %get-tuple-element.18.cos_ref, ...), custom_call_target="tpu_custom_call" | custom-call | tf_op jit(solution)/shard_map/channelize/pallas_call | solution.py:145
  53.2 124.4 %exchange.1 = (bf16[64,64,16,128]{3,2,1,0:T(8,128)(2,1)}, f32[8,16,128]{2,1,0:T(8,128)}) custom-call(bf16[8,2,64,16,128]{4,3,2,1,0:T(8,128)(2,1)} %channelize.1.spec_ref, f32[16,128]{1,0:T(8,128)} %pad.4.model_ref), custom_call_target="tpu_custom_call" | custom-call | tf_op jit(solution)/shard_map/exchange/pallas_call | solution.py:294
  177.6 0.7 dynamic-slice_bitcast_fusion
  178.3 0.2 broadcast_in_dim.7
  178.5 0.9 reshape.106.delay_ref
  179.4 16.0 %form_beams.1 = (f32[128,64,128]{2,1,0:T(8,128)}, f32[128,64,128]{2,1,0:T(8,128)}) custom-call(bf16[64,64,16,128]{3,2,1,0:T(8,128)(2,1)} %get-tuple-element.6.data_ref, f32[16,1024]{1,0:T(8,128)} %reshape.106.delay_ref, f32[16,1024]{1,0:T(8,128)} %reshape.107.gain_ref, f32[1,1024]{1,0:T(1,128)} %fusion.18.base_ref), custom_call_target="tpu_custom_call" | custom-call | tf_op jit(solution)/shard_map/form_beams/pallas_call | solution.py:358
  (13 shorter events, 0.4 us)
Async XLA Ops:
  0.6 5.8 %copy-start = (f32[64,64]{1,0:T(8,128)S(1)}, f32[64,64]{1,0:T(8,128)}, u32[]{:S(2)}) copy-start(f32[64,64]{1,0:T(8,128)} %param.10) | copy-start | bytes 49156

commit v3 on v2

--- a/solution.py
+++ b/solution.py
@@ -3,6 +3,7 @@
 
 import jax
 import jax.numpy as jnp
+import numpy as np
 from jax import lax
 from jax.experimental import pallas as pl
 from jax.experimental.pallas import tpu as pltpu
@@ -17,6 +18,7 @@
 VMEM_LIMIT = 56 * 1024 * 1024
 SEND_ORDER = (6, 1, 4, 2, 7, 3, 5)
 WAIT_ORDER = (1, 2, 3, 6, 4, 7, 5)
+EARLY = (((), ()), (((1, 0),), ((2, 0),)))
 
 SIN_COEF = (6.283185272447949, -41.34169703819964, 81.60502363802586, -76.70153767014536, 42.01607576124393, -14.86832274947347, 3.199338841413777)
 COS_COEF = (0.999999999885554, -19.739208743453883, 64.93938907589225, -85.45665831478402, 60.242131338256826, -26.404668186962848, 7.800131436606334, -1.4531123148805878)
@@ -35,27 +37,21 @@
 
 
 def dft_tables():
-    first_idx = jnp.arange(P_SIZE, dtype=jnp.int32)
-    second_idx = jnp.arange(Q, dtype=jnp.int32)
-    half_idx = jnp.arange(Q // 2, dtype=jnp.int32)
-    first_angle = (
-        TWO_PI / P_SIZE * (first_idx[:, None] * first_idx[None, :] % P_SIZE).astype(jnp.float32)
-    )
-    twist_angle = (
-        TWO_PI / (P_SIZE * Q) * (first_idx[:, None] * second_idx[None, :]).astype(jnp.float32)
-    )
-    second_angle = TWO_PI / Q * (second_idx[:, None] * half_idx[None, :] % Q).astype(jnp.float32)
-    first = jnp.concatenate((jnp.cos(first_angle), -jnp.sin(first_angle)), axis=0)
-    cos_two = jnp.cos(second_angle).T.reshape(-1, TILE_B, Q)
-    sin_two = jnp.sin(second_angle).T.reshape(-1, TILE_B, Q)
-    re_rows = jnp.concatenate((cos_two, sin_two), axis=2)
-    im_rows = jnp.concatenate((-sin_two, cos_two), axis=2)
-    second = jnp.stack((re_rows, im_rows), axis=1).reshape(Q, 2 * Q)
+    first_idx, second_idx, half_idx = np.arange(P_SIZE), np.arange(Q), np.arange(Q // 2)
+    first_angle = TWO_PI / P_SIZE * (first_idx[:, None] * first_idx[None, :] % P_SIZE)
+    twist_angle = TWO_PI / NFFT * (first_idx[:, None] * second_idx[None, :])
+    second_angle = TWO_PI / Q * (second_idx[:, None] * half_idx[None, :] % Q)
+    first = np.concatenate((np.cos(first_angle), -np.sin(first_angle)), axis=0)
+    cos_two = np.cos(second_angle).T.reshape(-1, TILE_B, Q)
+    sin_two = np.sin(second_angle).T.reshape(-1, TILE_B, Q)
+    re_rows = np.concatenate((cos_two, sin_two), axis=2)
+    im_rows = np.concatenate((-sin_two, cos_two), axis=2)
+    second = np.stack((re_rows, im_rows), axis=1).reshape(Q, 2 * Q)
     return (
-        first.astype(jnp.bfloat16),
-        jnp.cos(twist_angle),
-        jnp.sin(twist_angle),
-        second.astype(jnp.bfloat16),
+        jnp.asarray(first.astype(np.float32).astype(jnp.bfloat16)),
+        jnp.asarray(np.cos(twist_angle).astype(np.float32)),
+        jnp.asarray(np.sin(twist_angle).astype(np.float32)),
+        jnp.asarray(second.astype(np.float32).astype(jnp.bfloat16)),
     )
 
 
@@ -118,57 +114,22 @@
     lax.fori_loop(0, P_SIZE, body, 0, unroll=8)
 
 
-def channel_kernel(
-    frames, volt_ref, taps_ref, first_ref, cos_ref, sin_ref, second_ref, out_ref, filt, turn_re, turn_im
-):
-    pols = volt_ref.shape[1]
-    count = pols * frames
-    filter_station(volt_ref.at[0], taps_ref, filt, pols, frames, taps_ref.shape[0])
-    first_section(filt, first_ref, cos_ref, sin_ref, turn_re, turn_im, count)
-
-    def store(a, value):
-        out_ref[:, 0, a] = value.reshape(out_ref.shape[0], 2 * TILE_B, count)
-
-    second_section(second_ref, turn_re, turn_im, count, store)
-
-
-def channelize(voltages, fir_taps, tables):
-    stations, pols, samples = voltages.shape
-    tap_count = fir_taps.shape[0]
-    blocks = samples // NFFT
-    frames = blocks - tap_count + 1
-    count = pols * frames
-    tiles = P_SIZE // TILE_B
-    volts = voltages.reshape(stations, pols, blocks, P_SIZE, Q)
-    taps = fir_taps.reshape(tap_count, P_SIZE, Q)
-    whole = lambda shape: pl.BlockSpec(shape, lambda l: (0,) * len(shape))
-    return pl.pallas_call(
-        functools.partial(channel_kernel, frames),
-        grid=(stations,),
-        in_specs=[
-            pl.BlockSpec((1, pols, blocks, P_SIZE, Q), lambda l: (l, 0, 0, 0, 0)),
-            whole(taps.shape),
-        ]
-        + [whole(t.shape) for t in tables],
-        out_specs=pl.BlockSpec(
-            (tiles, 1, P_SIZE, 2 * TILE_B, count), lambda l: (0, l, 0, 0, 0)
-        ),
-        out_shape=jax.ShapeDtypeStruct((tiles, stations, P_SIZE, 2 * TILE_B, count), jnp.bfloat16),
-        scratch_shapes=[
-            pltpu.VMEM((count, P_SIZE, Q), jnp.bfloat16),
-            pltpu.VMEM((count * P_SIZE, Q), jnp.float32),
-            pltpu.VMEM((count * P_SIZE, Q), jnp.float32),
-        ],
-        compiler_params=pltpu.CompilerParams(vmem_limit_bytes=VMEM_LIMIT),
-        name="channelize",
-    )(volts, taps, *tables)
-
-
 def exchange_kernel(
-    spec_ref,
+    volt_hbm,
     model_ref,
+    taps_ref,
+    first_ref,
+    cos_ref,
+    sin_ref,
+    second_ref,
     data_ref,
     models_ref,
+    volts,
+    filt,
+    turn_re,
+    turn_im,
+    spec_ref,
+    volt_sem,
     direct_send,
     direct_recv,
     far_send,
@@ -181,8 +142,16 @@
     model_recv,
     local_sem,
 ):
+    locals_, pols, blocks = volt_hbm.shape[:3]
+    tap_count = taps_ref.shape[0]
+    frames = blocks - tap_count + 1
+    count = pols * frames
+    loads = [
+        pltpu.make_async_copy(volt_hbm.at[l], volts.at[l], volt_sem.at[l]) for l in range(locals_)
+    ]
+    for load in loads:
+        load.start()
     stn, beam = lax.axis_index("stn"), lax.axis_index("beam")
-    locals_ = spec_ref.shape[1]
     far = (beam + 2) % 4
     near = beam + 1 - 2 * (beam % 2)
 
@@ -218,13 +187,55 @@
     pl.semaphore_wait(barrier, len(peers))
 
     own_copies = [pltpu.make_async_copy(model_ref, models_ref.at[stn], local_sem.at[locals_])]
+    own_copies[0].start()
     direct, far_copy, near_copy, last_copy, model_copy = {}, {}, {}, {}, {}
+    for m in range(1, 8):
+        model_copy[m] = remote(
+            model_ref, models_ref.at[stn], model_send.at[m], model_recv.at[m], partner(m), beam
+        )
+
+    def pass_on(key):
+        m, l = key
+        far_copy[key].wait_recv()
+        place = data_ref.at[row(partner(m), far, l)]
+        last_copy[key] = remote(
+            place, place, last_send.at[m, l], last_recv.at[m, l], stn, near
+        )
+
+    waiting = []
+
+    def step(key):
+        m, l = key
+        place = data_ref.at[row(partner(m), beam, l)]
+        if m:
+            direct[key].wait_recv()
+            src = place
+        else:
+            src = spec_ref.at[stn, l]
+        far_copy[key] = remote(src, place, far_send.at[m, l], far_recv.at[m, l], stn, far)
+        near_copy[key] = remote(src, place, near_send.at[m, l], near_recv.at[m, l], stn, near)
+        if waiting:
+            pass_on(waiting.pop())
+        waiting.append(key)
+
     for l in range(locals_):
-        own_copies.append(
-            pltpu.make_async_copy(
-                spec_ref.at[stn, l], data_ref.at[row(stn, beam, l)], local_sem.at[l]
-            )
-        )
+        loads[l].wait()
+        filter_station(volts.at[l], taps_ref, filt, pols, frames, tap_count)
+        for key in EARLY[l][0]:
+            step(key)
+        first_section(filt, first_ref, cos_ref, sin_ref, turn_re, turn_im, count)
+        for key in EARLY[l][1]:
+            step(key)
+
+        def store(a, value):
+            spec_ref[:, l, a] = value.reshape(spec_ref.shape[0], 2 * TILE_B, count)
+
+        second_section(second_ref, turn_re, turn_im, count, store)
+        own = pltpu.make_async_copy(
+            spec_ref.at[stn, l], data_ref.at[row(stn, beam, l)], local_sem.at[l]
+        )
+        own.start()
+        own_copies.append(own)
         for m in SEND_ORDER:
             direct[m, l] = remote(
                 spec_ref.at[partner(m), l],
@@ -234,45 +245,14 @@
                 partner(m),
                 beam,
             )
-        if l == 0:
-            for m in range(1, 8):
-                model_copy[m] = remote(
-                    model_ref,
-                    models_ref.at[stn],
-                    model_send.at[m],
-                    model_recv.at[m],
-                    partner(m),
-                    beam,
-                )
-    for copy in own_copies:
-        copy.start()
-
-    def pass_on(key):
-        m, l = key
-        far_copy[key].wait_recv()
-        place = data_ref.at[row(partner(m), far, l)]
-        last_copy[key] = remote(
-            place, place, last_send.at[m, l], last_recv.at[m, l], stn, near
-        )
-
-    steps = [(m, l) for m in (0,) + WAIT_ORDER[:3] for l in range(locals_)]
+        step((0, l))
+    steps = [(m, l) for m in WAIT_ORDER[:3] for l in range(locals_)]
     steps += [(m, l) for l in range(locals_) for m in WAIT_ORDER[3:]]
-    before = None
     for key in steps:
-        m, l = key
-        place = data_ref.at[row(partner(m), beam, l)]
-        if m:
-            direct[key].wait_recv()
-            src = place
-        else:
-            src = spec_ref.at[stn, l]
-        far_copy[key] = remote(src, place, far_send.at[m, l], far_recv.at[m, l], stn, far)
-        near_copy[key] = remote(src, place, near_send.at[m, l], near_recv.at[m, l], stn, near)
-        if before is not None:
-            pass_on(before)
-        before = key
-    pass_on(before)
-    for key in steps:
+        if key not in far_copy:
+            step(key)
+    pass_on(waiting.pop())
+    for key in far_copy:
         near_copy[key].wait_recv()
         last_copy[key].wait_recv()
         far_copy[key].wait_send()
@@ -286,50 +266,95 @@
         copy.wait()
 
 
-def exchange(spectra, model):
-    stn_count, locals_ = spectra.shape[:2]
+def exchange(voltages, fir_taps, model, stn_count):
+    locals_, pols, samples = voltages.shape
+    tap_count = fir_taps.shape[0]
+    blocks = samples // NFFT
+    count = pols * (blocks - tap_count + 1)
     stations = stn_count * 4 * locals_
     pair = pltpu.SemaphoreType.DMA((stn_count, locals_))
     one = pltpu.SemaphoreType.DMA((stn_count,))
+    anywhere, vmem = pl.BlockSpec(memory_space=pl.ANY), pl.BlockSpec(memory_space=pltpu.VMEM)
     return pl.pallas_call(
         exchange_kernel,
-        in_specs=[pl.BlockSpec(memory_space=pl.ANY)] * 2,
-        out_specs=[pl.BlockSpec(memory_space=pl.ANY)] * 2,
+        in_specs=[anywhere] * 2 + [vmem] * 5,
+        out_specs=[anywhere] * 2,
         out_shape=[
-            jax.ShapeDtypeStruct((stations,) + spectra.shape[2:], spectra.dtype),
+            jax.ShapeDtypeStruct((stations, P_SIZE, 2 * TILE_B, count), jnp.bfloat16),
             jax.ShapeDtypeStruct((stn_count,) + model.shape, model.dtype),
         ],
-        scratch_shapes=[pair] * 8 + [one, one, pltpu.SemaphoreType.DMA((locals_ + 1,))],
+        scratch_shapes=[
+            pltpu.VMEM((locals_, pols, blocks, P_SIZE, Q), jnp.bfloat16),
+            pltpu.VMEM((count, P_SIZE, Q), jnp.bfloat16),
+            pltpu.VMEM((count * P_SIZE, Q), jnp.float32),
+            pltpu.VMEM((count * P_SIZE, Q), jnp.float32),
+            pltpu.VMEM((stn_count, locals_, P_SIZE, 2 * TILE_B, count), jnp.bfloat16),
+            pltpu.SemaphoreType.DMA((locals_,)),
+        ]
+        + [pair] * 8
+        + [one, one, pltpu.SemaphoreType.DMA((locals_ + 1,))],
         compiler_params=pltpu.CompilerParams(
             collective_id=0, has_side_effects=True, vmem_limit_bytes=VMEM_LIMIT
         ),
         name="exchange",
-    )(spectra, model)
-
-
-def beam_kernel(step_a, scale, data_ref, delay_ref, gain_ref, base_ref, re_ref, im_ref):
+    )(
+        voltages.reshape(locals_, pols, blocks, P_SIZE, Q),
+        model,
+        fir_taps.reshape(tap_count, P_SIZE, Q),
+        *dft_tables(),
+    )
+
+
+def beam_kernel(
+    step_a,
+    scale,
+    owners_ref,
+    order_ref,
+    data_ref,
+    models_ref,
+    taper_ref,
+    map_ref,
+    mask_ref,
+    re_ref,
+    im_ref,
+    rows_ref,
+    delay_ref,
+    gain_ref,
+):
     beams, lanes = delay_ref.shape
+    stations = map_ref.shape[1]
     count = data_ref.shape[-1]
-    lane = lax.broadcasted_iota(jnp.int32, (TILE_B, lanes), 1)
-    row = lax.broadcasted_iota(jnp.int32, (TILE_B, lanes), 0)
-    keep = lane % TILE_B == row
-    quarter = (lane[:1] // TILE_B % 2).astype(jnp.float32) * 0.25
+    stn, beam = lax.axis_index("stn"), lax.axis_index("beam")
+    step_idx = pl.program_id(0)
+
+    @pl.when(step_idx == 0)
+    def _():
+        phys = lax.broadcasted_iota(jnp.int32, (stations, stations), 0)
+        pick = (phys == map_ref[...]).astype(jnp.float32)
+        station = lax.broadcasted_iota(jnp.int32, (stations, lanes), 0)
+        lane_at = lax.broadcasted_iota(jnp.int32, (stations, lanes), 1)
+        widen = (lane_at // (2 * TILE_B) == station).astype(jnp.float32)
+
+        def by_lane(rows):
+            exact = functools.partial(
+                jnp.dot, precision=lax.Precision.HIGHEST, preferred_element_type=jnp.float32
+            )
+            return exact(exact(rows, pick), widen)
+
+        for j in range(beams):
+            rows_ref[pl.ds(j, 1), :] = taper_ref[pl.ds(order_ref[beam * beams + j], 1), :]
+        gain_ref[...] = by_lane(rows_ref[...])
+        delay_ref[...] = by_lane(models_ref[owners_ref[beam]])
+
+    lane = lax.broadcasted_iota(jnp.int32, (1, lanes), 1)
+    quarter = (lane // TILE_B % 2).astype(jnp.float32) * 0.25
+    chan = (P_SIZE * (TILE_B * stn + lane % TILE_B) + step_idx * step_a).astype(jnp.float32)
     delay = delay_ref[...]
-    chan = base_ref[...] + (pl.program_id(0) * step_a).astype(jnp.float32)
     sin_t, cos_t = sin_cos_turns(delay * chan * (1.0 / NFFT) - quarter)
     sin_d, cos_d = sin_cos_turns(delay * (1.0 / NFFT))
     part_re = gain_ref[...] * cos_t
     part_im = -(gain_ref[...] * sin_t)
-
-    def spread(part):
-        return (
-            jnp.where(keep[None], part[:, None, :], 0.0)
-            .astype(jnp.bfloat16)
-            .reshape(beams * TILE_B, lanes)
-        )
-
-    out_re = re_ref.reshape(beams * TILE_B * step_a, count)
-    out_im = im_ref.reshape(beams * TILE_B * step_a, count)
+    outs = [ref.reshape(beams * TILE_B * step_a, count) for ref in (re_ref, im_ref)]
     for a in range(step_a):
         if a:
             part_re, part_im = (
@@ -337,43 +362,56 @@
                 part_im * cos_d - part_re * sin_d,
             )
         data = data_ref[:, a].reshape(lanes, count)
-        rows = pl.ds(a, beams * TILE_B, stride=step_a)
-        out_re[rows, :] = (
-            jnp.dot(spread(part_re), data, preferred_element_type=jnp.float32) * scale
-        )
-        out_im[rows, :] = (
-            jnp.dot(spread(part_im), data, preferred_element_type=jnp.float32) * scale
-        )
-
-
-def form_beams(data, delay, gain, first_chan, scale):
+        weights = jnp.concatenate(
+            [
+                part.astype(jnp.bfloat16) * mask_ref[b]
+                for part in (part_re, part_im)
+                for b in range(TILE_B)
+            ],
+            axis=0,
+        )
+        formed = jnp.dot(weights, data, preferred_element_type=jnp.float32) * scale
+        for half, out in enumerate(outs):
+            for b in range(TILE_B):
+                first = (half * TILE_B + b) * beams
+                out[pl.ds(b * step_a + a, beams, stride=TILE_B * step_a), :] = formed[
+                    first : first + beams
+                ]
+
+
+def form_beams(data, models, taper, station_map, beam_order, owners, scale):
     stations, _, tile_rows, count = data.shape
-    beams = delay.shape[0]
+    beams = models.shape[1]
     lanes = stations * tile_rows
     step_a = 8
-    base = first_chan + P_SIZE * (jnp.arange(lanes, dtype=jnp.int32) % TILE_B)
-    spec = lambda shape: pl.BlockSpec(shape, lambda i: (0,) * len(shape))
+    mask = np.broadcast_to(
+        np.arange(lanes)[None, None] % TILE_B == np.arange(TILE_B)[:, None, None],
+        (TILE_B, beams, lanes),
+    )
+    whole = lambda x: pl.BlockSpec(x.shape, lambda i: (0,) * x.ndim)
+    smem = pl.BlockSpec(memory_space=pltpu.SMEM)
     out_spec = pl.BlockSpec((beams * TILE_B, step_a, count), lambda i: (0, i, 0))
     out_shape = jax.ShapeDtypeStruct((beams * TILE_B, P_SIZE, count), jnp.float32)
+    held = [models, taper, station_map[None], jnp.asarray(mask.astype(jnp.bfloat16))]
     re, im = pl.pallas_call(
         functools.partial(beam_kernel, step_a, scale),
         grid=(P_SIZE // step_a,),
         in_specs=[
+            smem,
+            smem,
             pl.BlockSpec((stations, step_a, tile_rows, count), lambda i: (0, i, 0, 0)),
-            spec((beams, lanes)),
-            spec((beams, lanes)),
-            spec((1, lanes)),
-        ],
+        ]
+        + [whole(x) for x in held],
         out_specs=[out_spec, out_spec],
         out_shape=[out_shape, out_shape],
+        scratch_shapes=[
+            pltpu.VMEM((beams, stations), jnp.float32),
+            pltpu.VMEM((beams, lanes), jnp.float32),
+            pltpu.VMEM((beams, lanes), jnp.float32),
+        ],
         compiler_params=pltpu.CompilerParams(vmem_limit_bytes=VMEM_LIMIT),
         name="form_beams",
-    )(
-        data,
-        jnp.repeat(delay, tile_rows, axis=1),
-        jnp.repeat(gain, tile_rows, axis=1),
-        base.astype(jnp.float32)[None],
-    )
+    )(owners, beam_order, data, *held)
     shape = (beams, TILE_B * P_SIZE, count)
     return re.reshape(shape), im.reshape(shape)
 
@@ -509,23 +547,15 @@
 def on_device(voltages, fir_taps, delays, taper, station_map, beam_order, owners):
     stn_count = lax.axis_size("stn")
     beam_count = lax.axis_size("beam")
-    stn_pos = lax.axis_index("stn")
-    beam_pos = lax.axis_index("beam")
-    local_stations = voltages.shape[0]
     stations = station_map.shape[0]
-    group_beams = beam_order.shape[0] // beam_count
     chan_dev = CHANNELS // stn_count
     if (stn_count, beam_count, chan_dev) != (8, 4, P_SIZE * TILE_B):
         return general_device(
             voltages, fir_taps, delays, taper, station_map, beam_order, owners
         )
     scale = 1.0 / math.sqrt(NFFT * stations)
-    slot_gain = taper[beam_order[beam_pos * group_beams + jnp.arange(group_beams, dtype=jnp.int32)]]
-    own_model = jnp.pad(delays[0][:, station_map], ((0, 0), (0, -stations % 128)))
-    spectra = channelize(voltages, fir_taps, dft_tables())
-    data, models = exchange(spectra, own_model)
-    model = models[owners[beam_pos]][:, :stations]
-    return form_beams(data, model, slot_gain[:, station_map], stn_pos * chan_dev, scale)
+    data, models = exchange(voltages, fir_taps, delays[0], stn_count)
+    return form_beams(data, models, taper, station_map, beam_order, owners, scale)
 
 
 def solution(mesh):

time: 196 us -> 167 us (0.85)
  Pallas kernels: 172 us -> 158 us
  local copies, waits for them, and re-layouts: 17.5 us -> 8.69 us
  other arithmetic: 3.73 us -> 0 us
  between operations: 2.66 us -> 0.64 us
    pallas_call x2 -> x1, Pallas kernels: 156 us -> 139 us  [exchange(): pl.pallas_call(exchange_kernel, in_specs=[anywhere] * 2 + [vmem] * 5, out...]
    gather x7 -> x0, local copies, waits for them, and re-layouts: 3.28 us -> none  [the longest x1 1.32 us: on_device(): beam_order[beam_pos * group_beams + jnp.arange(group_beams, dtype=jnp.int...]
    pallas_call x1, Pallas kernels: 16 us -> 18.9 us  [form_beams(): pl.pallas_call(functools.partial(beam_kernel, step_a, scale), grid=(P_SIZ...]
    reshape x4 -> x2, local copies, waits for them, and re-layouts: 9.36 us -> 7.55 us  [the longest x1 6.78 us: exchange(): voltages.reshape(locals_, pols, blocks, P_SIZE, Q)]
where the time goes in v3:
time: 167 us
  Pallas kernels  158 us (95%)
  local copies, waits for them, and re-layouts  8.69 us (5%)
    pallas_call x1, Pallas kernels, exchange(): pl.pallas_call(exchange_kernel, in_specs=[anywhere] * 2 + [vmem] * 5, out...  139 us
    pallas_call x1, Pallas kernels, form_beams(): pl.pallas_call(functools.partial(beam_kernel, step_a, scale), grid=(P_SIZ...  18.9 us
    reshape x1, local copies, waits for them, and re-layouts, exchange(): voltages.reshape(locals_, pols, blocks, P_SIZE, Q)  6.78 us

profile of v3, /device:TPU:9, one launch (start us, length us, event | category | flops | bytes accessed | tf_op | source)
XLA Modules:
  0.0 166.9 jit_solution(18072908665436702570)
XLA Ops:
  0.6 1.1 copy.14
  1.8 0.8 slice.taps_ref
  2.6 6.8 %reshape.16.volt_hbm = bf16[2,2,75,64,128]{4,3,2,1,0:T(8,128)(2,1)} reshape(bf16[2,2,614400]{2,1,0:T(2,128)(2,1)} %param.12) | data formatting | bytes 9830400 | tf_op jit(solution)/shard_map/reshape | solution.py:301
  9.3 138.7 %exchange.1 = (bf16[64,64,16,128]{3,2,1,0:T(8,128)(2,1)}, f32[8,16,64]{2,1,0:T(8,128)}) custom-call(bf16[2,2,75,64,128]{4,3,2,1,0:T(8,128)(2,1)} %reshape.16.volt_hbm, f32[16,64]{1,0:T(8,128)} %bitcast.9, f32[12,64,128]{2,1,0:T(8,128)} %slice.taps_ref, bf16[128,64]{1,0:T(8,128)(2,1)} %constant.10.clone.first_ref, f32[64,128]{1,0:T(8,128)} %constant.11.clone.cos_ref, ...), custom_call_target="tpu_custom_call" | custom-call | tf_op jit(solution)/shard_map/exchange/pallas_call | solution.py:278
  148.0 18.9 %form_beams.1 = (f32[128,64,128]{2,1,0:T(8,128)}, f32[128,64,128]{2,1,0:T(8,128)}) custom-call(s32[4]{0:T(128)} %owners_ref.1, s32[64]{0:T(128)} %order_ref.1, bf16[64,64,16,128]{3,2,1,0:T(8,128)(2,1)} %get-tuple-element.6.data_ref, f32[8,16,64]{2,1,0:T(8,128)} %get-tuple-element.7.models_ref, f32[64,64]{1,0:T(8,128)} %taper_ref.1, s32[1,64]{1,0:T(1,128)} %bitcast.10, ...), custom_call_target="tpu_custom_call" | custom-call | tf_op jit(solution)/shard_map/form_beams/pallas_call | solution.py:396

commit v4 on v3

--- a/solution.py
+++ b/solution.py
@@ -15,6 +15,7 @@
 NFFT = P_SIZE * Q
 TILE_B = 8
 TWO_PI = 2.0 * math.pi
+PITCH = P_SIZE + 8
 VMEM_LIMIT = 56 * 1024 * 1024
 SEND_ORDER = (6, 1, 4, 2, 7, 3, 5)
 WAIT_ORDER = (1, 2, 3, 6, 4, 7, 5)
@@ -89,19 +90,19 @@
         for i in range(width):
             re = both[:P_SIZE, i * Q : (i + 1) * Q]
             im = both[P_SIZE:, i * Q : (i + 1) * Q]
-            rows = pl.ds(pl.multiple_of((c0 + i) * P_SIZE, P_SIZE), P_SIZE)
+            rows = pl.ds(pl.multiple_of((c0 + i) * PITCH, 8), P_SIZE)
             turn_re[rows, :] = re * cos_ref[...] + im * sin_ref[...]
             turn_im[rows, :] = im * cos_ref[...] - re * sin_ref[...]
         return carry
 
-    lax.fori_loop(0, count // width, body, 0, unroll=2)
+    lax.fori_loop(0, count // width, body, 0, unroll=4)
 
 
 def second_section(second_ref, turn_re, turn_im, count, store):
     table = second_ref[...]
 
     def body(a, carry):
-        rows = pl.ds(a, count, stride=P_SIZE)
+        rows = pl.ds(a, count, stride=PITCH)
         turned = jnp.concatenate(
             (turn_re[rows, :].astype(jnp.bfloat16), turn_im[rows, :].astype(jnp.bfloat16)), axis=1
         )
@@ -246,8 +247,7 @@
                 beam,
             )
         step((0, l))
-    steps = [(m, l) for m in WAIT_ORDER[:3] for l in range(locals_)]
-    steps += [(m, l) for l in range(locals_) for m in WAIT_ORDER[3:]]
+    steps = [(m, l) for l in range(locals_) for m in WAIT_ORDER]
     for key in steps:
         if key not in far_copy:
             step(key)
@@ -286,8 +286,8 @@
         scratch_shapes=[
             pltpu.VMEM((locals_, pols, blocks, P_SIZE, Q), jnp.bfloat16),
             pltpu.VMEM((count, P_SIZE, Q), jnp.bfloat16),
-            pltpu.VMEM((count * P_SIZE, Q), jnp.float32),
-            pltpu.VMEM((count * P_SIZE, Q), jnp.float32),
+            pltpu.VMEM((count * PITCH, Q), jnp.float32),
+            pltpu.VMEM((count * PITCH, Q), jnp.float32),
             pltpu.VMEM((stn_count, locals_, P_SIZE, 2 * TILE_B, count), jnp.bfloat16),
             pltpu.SemaphoreType.DMA((locals_,)),
         ]
@@ -320,6 +320,8 @@
     rows_ref,
     delay_ref,
     gain_ref,
+    held_re,
+    held_im,
 ):
     beams, lanes = delay_ref.shape
     stations = map_ref.shape[1]
@@ -330,21 +332,27 @@
     @pl.when(step_idx == 0)
     def _():
         phys = lax.broadcasted_iota(jnp.int32, (stations, stations), 0)
-        pick = (phys == map_ref[...]).astype(jnp.float32)
+        pick = (phys == map_ref[...]).astype(jnp.float32).astype(jnp.bfloat16)
         station = lax.broadcasted_iota(jnp.int32, (stations, lanes), 0)
         lane_at = lax.broadcasted_iota(jnp.int32, (stations, lanes), 1)
-        widen = (lane_at // (2 * TILE_B) == station).astype(jnp.float32)
-
-        def by_lane(rows):
-            exact = functools.partial(
-                jnp.dot, precision=lax.Precision.HIGHEST, preferred_element_type=jnp.float32
-            )
-            return exact(exact(rows, pick), widen)
-
+        widen = (lane_at // (2 * TILE_B) == station).astype(jnp.float32).astype(jnp.bfloat16)
+
+        spread = jnp.dot(pick, widen, preferred_element_type=jnp.float32).astype(jnp.bfloat16)
         for j in range(beams):
             rows_ref[pl.ds(j, 1), :] = taper_ref[pl.ds(order_ref[beam * beams + j], 1), :]
-        gain_ref[...] = by_lane(rows_ref[...])
-        delay_ref[...] = by_lane(models_ref[owners_ref[beam]])
+        both = jnp.concatenate((models_ref[owners_ref[beam]], rows_ref[...]), axis=0)
+        high = both.astype(jnp.bfloat16)
+        rest = both - high.astype(jnp.float32)
+        middle = rest.astype(jnp.bfloat16)
+        low = (rest - middle.astype(jnp.float32)).astype(jnp.bfloat16)
+        picked = jnp.dot(
+            jnp.concatenate((high, middle, low), axis=0),
+            spread,
+            preferred_element_type=jnp.float32,
+        )
+        held = picked[: 2 * beams] + picked[2 * beams : 4 * beams] + picked[4 * beams :]
+        delay_ref[...] = held[:beams]
+        gain_ref[...] = held[beams:]
 
     lane = lax.broadcasted_iota(jnp.int32, (1, lanes), 1)
     quarter = (lane // TILE_B % 2).astype(jnp.float32) * 0.25
@@ -354,7 +362,7 @@
     sin_d, cos_d = sin_cos_turns(delay * (1.0 / NFFT))
     part_re = gain_ref[...] * cos_t
     part_im = -(gain_ref[...] * sin_t)
-    outs = [ref.reshape(beams * TILE_B * step_a, count) for ref in (re_ref, im_ref)]
+    pitch = held_re.shape[0] // beams
     for a in range(step_a):
         if a:
             part_re, part_im = (
@@ -371,12 +379,15 @@
             axis=0,
         )
         formed = jnp.dot(weights, data, preferred_element_type=jnp.float32) * scale
-        for half, out in enumerate(outs):
+        for half, out in enumerate((held_re, held_im)):
             for b in range(TILE_B):
                 first = (half * TILE_B + b) * beams
-                out[pl.ds(b * step_a + a, beams, stride=TILE_B * step_a), :] = formed[
-                    first : first + beams
-                ]
+                out[pl.ds(b * step_a + a, beams, stride=pitch), :] = formed[first : first + beams]
+    for held, out in ((held_re, re_ref), (held_im, im_ref)):
+        for j in range(beams):
+            out[pl.ds(j * TILE_B, TILE_B)] = held[
+                pl.ds(j * pitch, TILE_B * step_a), :
+            ].reshape(TILE_B, step_a, count)
 
 
 def form_beams(data, models, taper, station_map, beam_order, owners, scale):
@@ -408,6 +419,8 @@
             pltpu.VMEM((beams, stations), jnp.float32),
             pltpu.VMEM((beams, lanes), jnp.float32),
             pltpu.VMEM((beams, lanes), jnp.float32),
+            pltpu.VMEM((beams * (TILE_B + 1) * step_a, count), jnp.float32),
+            pltpu.VMEM((beams * (TILE_B + 1) * step_a, count), jnp.float32),
         ],
         compiler_params=pltpu.CompilerParams(vmem_limit_bytes=VMEM_LIMIT),
         name="form_beams",

time: 167 us -> 156 us (0.934)
  the two profiles are of different devices: /device:TPU:9 before, /device:TPU:0 now
where the time goes in v4:
time: 156 us
  Pallas kernels  146 us (94%)
  local copies, waits for them, and re-layouts  8.69 us (6%)
    pallas_call x1, Pallas kernels, exchange(): pl.pallas_call(exchange_kernel, in_specs=[anywhere] * 2 + [vmem] * 5, out...  130 us
    pallas_call x1, Pallas kernels, form_beams(): pl.pallas_call(functools.partial(beam_kernel, step_a, scale), grid=(P_SIZ...  16.1 us
    reshape x1, local copies, waits for them, and re-layouts, exchange(): voltages.reshape(locals_, pols, blocks, P_SIZE, Q)  6.78 us

profile of v4, /device:TPU:0, one launch (start us, length us, event | category | flops | bytes accessed | tf_op | source)
XLA Modules:
  0.0 155.5 jit_solution(1523793541647655345)
XLA Ops:
  0.6 1.1 copy.14
  1.8 0.8 slice.taps_ref
  2.6 6.8 %reshape.16.volt_hbm = bf16[2,2,75,64,128]{4,3,2,1,0:T(8,128)(2,1)} reshape(bf16[2,2,614400]{2,1,0:T(2,128)(2,1)} %param.12) | data formatting | bytes 9830400 | tf_op jit(solution)/shard_map/reshape | solution.py:301
  9.3 130.1 %exchange.1 = (bf16[64,64,16,128]{3,2,1,0:T(8,128)(2,1)}, f32[8,16,64]{2,1,0:T(8,128)}) custom-call(bf16[2,2,75,64,128]{4,3,2,1,0:T(8,128)(2,1)} %reshape.16.volt_hbm, f32[16,64]{1,0:T(8,128)} %bitcast.9, f32[12,64,128]{2,1,0:T(8,128)} %slice.taps_ref, bf16[128,64]{1,0:T(8,128)(2,1)} %constant.10.clone.first_ref, f32[64,128]{1,0:T(8,128)} %constant.11.clone.cos_ref, ...), custom_call_target="tpu_custom_call" | custom-call | tf_op jit(solution)/shard_map/exchange/pallas_call | solution.py:278
  139.4 16.1 %form_beams.1 = (f32[128,64,128]{2,1,0:T(8,128)}, f32[128,64,128]{2,1,0:T(8,128)}) custom-call(s32[4]{0:T(128)} %owners_ref.1, s32[64]{0:T(128)} %order_ref.1, bf16[64,64,16,128]{3,2,1,0:T(8,128)(2,1)} %get-tuple-element.6.data_ref, f32[8,16,64]{2,1,0:T(8,128)} %get-tuple-element.7.models_ref, f32[64,64]{1,0:T(8,128)} %taper_ref.1, s32[1,64]{1,0:T(1,128)} %bitcast.10, ...), custom_call_target="tpu_custom_call" | custom-call | tf_op jit(solution)/shard_map/form_beams/pallas_call | solution.py:407

commit v5 on v4

--- a/solution.py
+++ b/solution.py
@@ -17,8 +17,8 @@
 TWO_PI = 2.0 * math.pi
 PITCH = P_SIZE + 8
 VMEM_LIMIT = 56 * 1024 * 1024
-SEND_ORDER = (6, 1, 4, 2, 7, 3, 5)
-WAIT_ORDER = (1, 2, 3, 6, 4, 7, 5)
+SEND_ORDER = (1, 6, 2, 4, 3, 7, 5)
+WAIT_ORDER = (1, 2, 6, 3, 4, 7, 5)
 EARLY = (((), ()), (((1, 0),), ((2, 0),)))
 
 SIN_COEF = (6.283185272447949, -41.34169703819964, 81.60502363802586, -76.70153767014536, 42.01607576124393, -14.86832274947347, 3.199338841413777)
@@ -60,7 +60,7 @@
     group = 8
     for part in range(P_SIZE // 16):
         rows = pl.ds(part * 16, 16)
-        taps = [taps_ref[m, rows, :] for m in range(tap_count)]
+        taps = [taps_ref[pl.ds(m * PITCH + part * 16, 16), :] for m in range(tap_count)]
 
         def body(idx, carry):
             pol, first = idx // (frames // group), idx % (frames // group) * group
@@ -118,7 +118,7 @@
 def exchange_kernel(
     volt_hbm,
     model_ref,
-    taps_ref,
+    flat_taps_ref,
     first_ref,
     cos_ref,
     sin_ref,
@@ -130,6 +130,7 @@
     turn_re,
     turn_im,
     spec_ref,
+    taps_ref,
     volt_sem,
     direct_send,
     direct_recv,
@@ -144,7 +145,7 @@
     local_sem,
 ):
     locals_, pols, blocks = volt_hbm.shape[:3]
-    tap_count = taps_ref.shape[0]
+    tap_count = flat_taps_ref.shape[0]
     frames = blocks - tap_count + 1
     count = pols * frames
     loads = [
@@ -152,6 +153,8 @@
     ]
     for load in loads:
         load.start()
+    for n1 in range(P_SIZE):
+        taps_ref[pl.ds(n1, tap_count, stride=PITCH), :] = flat_taps_ref[:, n1 * Q : (n1 + 1) * Q]
     stn, beam = lax.axis_index("stn"), lax.axis_index("beam")
     far = (beam + 2) % 4
     near = beam + 1 - 2 * (beam % 2)
@@ -289,6 +292,7 @@
             pltpu.VMEM((count * PITCH, Q), jnp.float32),
             pltpu.VMEM((count * PITCH, Q), jnp.float32),
             pltpu.VMEM((stn_count, locals_, P_SIZE, 2 * TILE_B, count), jnp.bfloat16),
+            pltpu.VMEM((tap_count * PITCH, Q), jnp.float32),
             pltpu.SemaphoreType.DMA((locals_,)),
         ]
         + [pair] * 8
@@ -300,7 +304,7 @@
     )(
         voltages.reshape(locals_, pols, blocks, P_SIZE, Q),
         model,
-        fir_taps.reshape(tap_count, P_SIZE, Q),
+        fir_taps,
         *dft_tables(),
     )
 

time: 156 us -> 148 us (0.949)
  the two profiles are of different devices: /device:TPU:0 before, /device:TPU:9 now
where the time goes in v5:
time: 148 us; the launch traced here: 146 us
  Pallas kernels  138 us (93%)
  local copies, waits for them, and re-layouts  6.78 us (5%)
    pallas_call x1, Pallas kernels, exchange(): pl.pallas_call(exchange_kernel, in_specs=[anywhere] * 2 + [vmem] * 5, out...  122 us
    pallas_call x1, Pallas kernels, form_beams(): pl.pallas_call(functools.partial(beam_kernel, step_a, scale), grid=(P_SIZ...  16.1 us
    reshape x1, local copies, waits for them, and re-layouts, exchange(): voltages.reshape(locals_, pols, blocks, P_SIZE, Q)  6.78 us

profile of v5, /device:TPU:9, one launch (start us, length us, event | category | flops | bytes accessed | tf_op | source)
XLA Modules:
  0.0 145.6 jit_solution(4717123587980280895)
XLA Ops:
  0.6 6.8 %reshape.13.volt_hbm = bf16[2,2,75,64,128]{4,3,2,1,0:T(8,128)(2,1)} reshape(bf16[2,2,614400]{2,1,0:T(2,128)(2,1)} %param.12) | data formatting | bytes 9830400 | tf_op jit(solution)/shard_map/reshape | solution.py:305
  7.4 122.0 %exchange.1 = (bf16[64,64,16,128]{3,2,1,0:T(8,128)(2,1)}, f32[8,16,64]{2,1,0:T(8,128)}) custom-call(bf16[2,2,75,64,128]{4,3,2,1,0:T(8,128)(2,1)} %reshape.13.volt_hbm, f32[16,64]{1,0:T(8,128)} %bitcast.4, f32[12,8192]{1,0:T(8,128)} %flat_taps_ref.1, bf16[128,64]{1,0:T(8,128)(2,1)} %constant.10.clone.first_ref, f32[64,128]{1,0:T(8,128)} %constant.11.clone.cos_ref, ...), custom_call_target="tpu_custom_call" | custom-call | tf_op jit(solution)/shard_map/exchange/pallas_call | solution.py:281
  129.4 16.1 %form_beams.1 = (f32[128,64,128]{2,1,0:T(8,128)}, f32[128,64,128]{2,1,0:T(8,128)}) custom-call(s32[4]{0:T(128)} %owners_ref.1, s32[64]{0:T(128)} %order_ref.1, bf16[64,64,16,128]{3,2,1,0:T(8,128)(2,1)} %get-tuple-element.6.data_ref, f32[8,16,64]{2,1,0:T(8,128)} %get-tuple-element.7.models_ref, f32[64,64]{1,0:T(8,128)} %taper_ref.1, s32[1,64]{1,0:T(1,128)} %bitcast.5, ...), custom_call_target="tpu_custom_call" | custom-call | tf_op jit(solution)/shard_map/form_beams/pallas_call | solution.py:411
